TPU v7x, 512 devices: a whole 4x4x16 slice. The times are simulated.
512 devices in a mesh: dp: 32 (over x, z_lo), tensor: 16 (over y, z_hi, core).
Axes of the slice: x: 4, y: 4, z: 16 (z_hi: 2, z_lo: 8; z = z_hi * 8 + z_lo), core: 2. Of those that a mesh axis runs over, the one named last changes fastest.
Arguments:
- owner_states: float32 [64, 32, 128, 128], P('dp', 'tensor'), may hold values from -6 to 6
- sample_slot: int32 [1024], P('dp'), may hold values from 0 to 1023, each once
- query_in: bfloat16 [1024, 4, 2048], P('dp', None, 'tensor'), may hold values from -6 to 6
- key_in: bfloat16 [1024, 4, 2048], P('dp', None, 'tensor'), may hold values from -6 to 6
- value_in: bfloat16 [1024, 4, 4096], P('dp', None, 'tensor'), may hold values from -6 to 6
- gate_in: bfloat16 [1024, 4, 4096], P('dp', None, 'tensor'), may hold values from -6 to 6
- decay_in: float32 [1024, 4, 2, 32], P('dp', None, None, 'tensor'), may hold values from -6 to 6
- decay_rate: float32 [32], P('tensor'), may hold values from 0.05 to 2
- dt_bias: float32 [32], P('tensor'), may hold values from -4 to 4
- norm_gain: float32 [128], replicated, may hold values from 0.25 to 1.75
- out_weight: bfloat16 [4096, 2048], P('tensor'), may hold values from -0.09375 to 0.09375
Outputs:
- mixed: bfloat16 [1024, 4, 2048], P('dp', None, 'tensor')
- final_states: bfloat16 [1024, 32, 128, 128], P('dp', 'tensor')
Inputs may be any that keep to these rules, and one draw needn't show every extreme that they name: `sample_slot`: each slot appears once, so each prompt has exactly 16 rows, placed anywhere.
All inputs are finite; a program needn't handle non-finite values.
Results may differ from a plain program's by a relative error of at most 0.0049.
Values sent between devices are 32-bit elements; how exact they have to be, the bound alone decides.
A program may use at most 64 MiB of HBM per device.

v0:
```python
import jax
import jax.numpy as jnp
from jax import lax
from jax.sharding import PartitionSpec as P

DK = 128
DV = 128
SAMPLES = 16


def unit_rows(values):
    return values / jnp.sqrt(jnp.sum(values * values, axis=-1, keepdims=True) + 1e-06)


def body(
    owner_states,
    sample_slot,
    query_in,
    key_in,
    value_in,
    gate_in,
    decay_in,
    decay_rate,
    dt_bias,
    norm_gain,
    out_weight,
):
    rows = sample_slot.shape[0]
    steps = query_in.shape[1]
    heads = decay_rate.shape[0]
    prompt = sample_slot // SAMPLES
    queries = unit_rows(query_in.astype(jnp.float32).reshape(rows, steps, -1, DK)) / jnp.sqrt(
        jnp.float32(DK)
    )
    keys_all = unit_rows(key_in.astype(jnp.float32).reshape(rows, steps, -1, DK))
    queries = jnp.repeat(queries, 2, axis=2)
    keys_all = jnp.repeat(keys_all, 2, axis=2)
    values = value_in.astype(jnp.float32).reshape(rows, steps, heads, DV)
    gates = gate_in.astype(jnp.float32).reshape(rows, steps, heads, DV)
    beta = jax.nn.sigmoid(decay_in[:, :, 1])
    alpha = jnp.exp(-decay_rate * jax.nn.softplus(decay_in[:, :, 0] + dt_bias))
    every_state = lax.all_gather(owner_states, "dp", axis=0, tiled=True)
    start_state = jnp.take(every_state, prompt, axis=0)
    state = start_state
    outputs = []
    for advance_step in range(steps):
        state = alpha[:, advance_step, 0 : 0 + heads, None, None] * state
        key_now = keys_all[:, advance_step, 0 : 0 + heads]
        recalled = jnp.einsum("bhvk,bhk->bhv", state, key_now, precision=lax.Precision.HIGHEST)
        error = values[:, advance_step, 0 : 0 + heads] - recalled
        state = (
            state
            + beta[:, advance_step, 0 : 0 + heads, None, None]
            * error[:, :, :, None]
            * key_now[:, :, None, :]
        )
        outputs.append(
            jnp.einsum(
                "bhvk,bhk->bhv",
                state,
                queries[:, advance_step, 0 : 0 + heads],
                precision=lax.Precision.HIGHEST,
            )
        )
    output = jnp.stack(outputs, axis=1)
    scale = lax.rsqrt(jnp.mean(output * output, axis=-1, keepdims=True) + 1e-06)
    hidden = (
        (output * scale * norm_gain * jax.nn.silu(gates))
        .astype(jnp.bfloat16)
        .reshape(rows, steps, heads * DV)
    )
    shares = []
    for step in range(steps):
        term = jnp.dot(hidden[:, step], out_weight, preferred_element_type=jnp.float32)
        shares.append(lax.psum_scatter(term, "tensor", scatter_dimension=1, tiled=True))
    mixed = jnp.stack(shares, axis=1)
    return (mixed.astype(jnp.bfloat16), state.astype(jnp.bfloat16))


def solution(mesh):
    return jax.shard_map(
        body,
        mesh=mesh,
        in_specs=(
            P("dp", "tensor", None, None),
            P("dp"),
            P("dp", None, "tensor"),
            P("dp", None, "tensor"),
            P("dp", None, "tensor"),
            P("dp", None, "tensor"),
            P("dp", None, None, "tensor"),
            P("tensor"),
            P("tensor"),
            P(),
            P("tensor", None),
        ),
        out_specs=(P("dp", None, "tensor"), P("dp", "tensor", None, None)),
        check_vma=False,
    )
```

profile of v0, /device:TPU:6, one launch (start us, length us, event | category | flops | bytes accessed | tf_op | source)
XLA Modules:
  0.0 737.9 jit_solution(8653580709199083601)
XLA Ops:
  7.2 0.7 all-gather.2.cloned.1.call-update
  8.6 0.8 fusion.48
  9.5 0.7 divide_bitcast_fusion
  10.8 0.9 reshape.150
  11.7 0.7 compare_and_fusion
  12.4 0.9 fusion.34
  13.3 0.9 fusion.33
  14.9 0.9 convert_divide_fusion.1
  15.7 0.9 fusion.32
  16.7 237.2 %all-gather.2.cloned.1.call-done = f32[64,2,128,128]{3,2,1,0:T(8,128)} async-done(((f32[2,2,128,128]{3,2,1,0:T(8,128)}), f32[64,2,128,128]{3,2,1,0:T(8,128)}) %all-gather.2.cloned.1.call-update) | async-done | bytes 8388624 | tf_op jit(solution)/shard_map/all_gather | solution.py:42
  254.0 6.1 gather_fusion
  260.1 8.9 %fusion.6 = f32[32,2,1,128]{3,2,1,0:T(1,128)S(1)} fusion(f32[32,2,128,1]{2,3,1,0:T(1,128)S(1)} %bitcast.151, f32[32,2,128,128]{3,2,1,0:T(8,128)} %gather_fusion, f32[32,2]{1,0:T(8,128)S(1)} %copy.69, pred[32]{0:T(512)(128)(4,1)S(1)} %get-tuple-element.12), kind=kOutput, calls=%fused_computation.12 | convolution fusion | flops 14680064 | bytes 4260128 | tf_op jit(solution)/shard_map/bhvk,bhk->bhv/dot_general | solution.py:49
  269.2 6.9 fusion.51
  276.1 7.1 fusion.4
  283.3 8.7 %fusion.9 = f32[32,2,1,128]{3,2,1,0:T(1,128)S(1)} fusion(f32[32,2,128,1]{2,3,1,0:T(1,128)S(1)} %bitcast.168, f32[32,128]{1,0:T(8,128)S(1)} %bitcast.144, f32[32,2,128]{2,1,0:T(2,128)S(1)} %fusion.40, f32[32,2]{1,0:T(8,128)S(1)} %copy.72, f32[32,2,128,128]{3,2,1,0:T(8,128)S(1)} %copy-done.1, f32[32,128]{1,0:T(8,128)S(1)} %bitcast.129, ...), kind=kOutput, calls=%fused_computation.15 | convolution fusion | flops 19922944 | bytes 4358688 | tf_op jit(solution)/shard_map/bhvk,bhk->bhv/dot_general | solution.py:58
  292.1 9.4 %fusion.2 = f32[32,2,1,128]{3,2,1,0:T(1,128)S(1)} fusion(f32[32,2,128,1]{2,3,1,0:T(1,128)S(1)} %bitcast.172, f32[32,2]{1,0:T(8,128)S(1)} %copy.75, f32[32,128]{1,0:T(8,128)S(1)} %bitcast.145, f32[32,2,128]{2,1,0:T(2,128)S(1)} %fusion.40, f32[32,2]{1,0:T(8,128)S(1)} %copy.72, f32[32,2,128,128]{3,2,1,0:T(8,128)S(1)} %copy-done.1, f32[32,128]{1,0:T(8,128)S(1)} %bitcast.130, ...), kind=kOutput, calls=%fused_computation.8 | convolution fusion | flops 20971520 | bytes 4358944 | tf_op jit(solution)/shard_map/bhvk,bhk->bhv/dot_general | solution.py:49
  301.6 10.5 %fusion.50 = f32[32,2,1,128]{3,2,1,0:T(1,128)S(1)} fusion(f32[32,2,128,1]{2,3,1,0:T(1,128)S(1)} %bitcast.169, f32[32,128]{1,0:T(8,128)S(1)} %bitcast.139, f32[32,2,128]{2,1,0:T(2,128)S(1)} %fusion.38, f32[32,2]{1,0:T(8,128)S(1)} %copy.75, f32[32,128]{1,0:T(8,128)S(1)} %bitcast.146, f32[32,2,128]{2,1,0:T(2,128)S(1)} %fusion.40, f32[32,2]{1,0:T(8,128)S(1)} %copy.72, ...), kind=kOutput, calls=%fused_computation.99 | convolution fusion | flops 23068672 | bytes 4408096 | tf_op jit(solution)/shard_map/bhvk,bhk->bhv/dot_general | solution.py:58
  312.1 10.5 %fusion = f32[32,2,1,128]{3,2,1,0:T(1,128)S(1)} fusion(f32[32,2,128,1]{2,3,1,0:T(1,128)S(1)} %bitcast.173, f32[32,2]{1,0:T(8,128)S(1)} %copy.78, f32[32,128]{1,0:T(8,128)S(1)} %bitcast.140, f32[32,2,128]{2,1,0:T(2,128)S(1)} %fusion.38, f32[32,2]{1,0:T(8,128)S(1)} %copy.75, f32[32,128]{1,0:T(8,128)S(1)} %bitcast.147, f32[32,2,128]{2,1,0:T(2,128)S(1)} %fusion.40, ...), kind=kOutput, calls=%fused_computation.6 | convolution fusion | flops 24117248 | bytes 4408352 | tf_op jit(solution)/shard_map/bhvk,bhk->bhv/dot_general | solution.py:49
  322.8 13.2 %fusion.8 = f32[32,2,1,128]{3,2,1,0:T(1,128)S(1)} fusion(f32[32,2,128,1]{2,3,1,0:T(1,128)S(1)} %bitcast.170, f32[32,128]{1,0:T(8,128)S(1)} %bitcast.136, f32[32,2,128]{2,1,0:T(2,128)S(1)} %fusion.36, f32[32,2]{1,0:T(8,128)S(1)} %copy.78, f32[32,128]{1,0:T(8,128)S(1)} %bitcast.141, f32[32,2,128]{2,1,0:T(2,128)S(1)} %fusion.38, f32[32,2]{1,0:T(8,128)S(1)} %copy.75, ...), kind=kOutput, calls=%fused_computation.14 | convolution fusion | flops 26214400 | bytes 4457504 | tf_op jit(solution)/shard_map/bhvk,bhk->bhv/dot_general | solution.py:58
  336.8 1.0 fusion.43
  337.9 1.0 fusion.44
  339.0 1.0 fusion.45
  340.0 8.7 %fusion.7 = bf16[32,2,128,128]{3,2,1,0:T(8,128)(2,1)} fusion(f32[32,128]{1,0:T(8,128)S(1)} %bitcast.137, f32[32,2,128]{2,1,0:T(2,128)S(1)} %fusion.36, f32[32,2]{1,0:T(8,128)S(1)} %copy.78, f32[32,128]{1,0:T(8,128)S(1)} %bitcast.142, f32[32,2,128]{2,1,0:T(2,128)S(1)} %fusion.38, f32[32,128]{1,0:T(8,128)S(1)} %bitcast.149, f32[32,2,128]{2,1,0:T(2,128)S(1)} %fusion.40, ...), kind=kLoop, calls=%fused_computation.13 | loop fusion | flops 14680064 | bytes 6489120 | tf_op jit(solution)/shard_map/convert_element_type | solution.py:77
  348.8 1.0 fusion.46
  349.8 99.7 %reduce-scatter.11.cloned.1.call-done = f32[32,128]{1,0:T(8,128)} async-done(((f32[32,2048]{1,0:T(8,128)}), f32[32,128]{1,0:T(8,128)}) %reduce-scatter.11.cloned.1.call-update) | async-done | bytes 16400 | tf_op jit(solution)/shard_map/reduce_scatter | solution.py:75
  449.4 0.7 convert_bitcast_fusion
  450.2 93.1 %reduce-scatter.9.cloned.1.call-done = f32[32,128]{1,0:T(8,128)} async-done(((f32[32,2048]{1,0:T(8,128)}), f32[32,128]{1,0:T(8,128)}) %reduce-scatter.9.cloned.1.call-update) | async-done | bytes 16400 | tf_op jit(solution)/shard_map/reduce_scatter | solution.py:75
  543.3 0.7 convert_bitcast_fusion.1
  544.0 92.3 %reduce-scatter.7.cloned.1.call-done = f32[32,128]{1,0:T(8,128)} async-done(((f32[32,2048]{1,0:T(8,128)}), f32[32,128]{1,0:T(8,128)}) %reduce-scatter.7.cloned.1.call-update) | async-done | bytes 16400 | tf_op jit(solution)/shard_map/reduce_scatter | solution.py:75
  636.3 0.7 convert_bitcast_fusion.2
  637.0 92.9 %reduce-scatter.5.cloned.1.call-done = f32[32,128]{1,0:T(8,128)} async-done(((f32[32,2048]{1,0:T(8,128)}), f32[32,128]{1,0:T(8,128)}) %reduce-scatter.5.cloned.1.call-update) | async-done | bytes 16400 | tf_op jit(solution)/shard_map/reduce_scatter | solution.py:75
  730.0 0.7 convert_bitcast_fusion.3
  (55 shorter events, 4.3 us)
Async XLA Ops:
  7.2 329.7 %copy-start = (bf16[256,2048]{1,0:T(8,128)(2,1)S(1)}, bf16[256,2048]{1,0:T(8,128)(2,1)}, u32[]{:S(2)}) copy-start(bf16[256,2048]{1,0:T(8,128)(2,1)} %param.21) | copy-start | bytes 3145732
  7.2 246.8 %all-gather.2.cloned.1.call-start = ((), (), s32[]{:S(2)}) async-start(), calls=%async_computation.4 | async-start | bytes 8650752 | tf_op jit(solution)/shard_map/all_gather | solution.py:42
  7.9 441.5 %reduce-scatter.11.cloned.1.call-start = ((), (), s32[]{:S(2)}) async-start(), calls=%async_computation.8 | async-start | bytes 278528 | tf_op jit(solution)/shard_map/reduce_scatter | solution.py:75
  260.1 9.0 %copy-start.1 = (f32[32,2,128,128]{3,2,1,0:T(8,128)S(1)}, f32[32,2,128,128]{3,2,1,0:T(8,128)}, u32[]{:S(2)}) copy-start(f32[32,2,128,128]{3,2,1,0:T(8,128)} %gather_fusion) | copy-start | bytes 12582916
  322.8 14.0 %copy-start.2 = (bf16[32,4,256]{2,1,0:T(4,128)(2,1)S(1)}, bf16[32,4,256]{2,1,0:T(4,128)(2,1)}, u32[]{:S(2)}) copy-start(bf16[32,4,256]{2,1,0:T(4,128)(2,1)} %param.16) | copy-start | bytes 196612
  337.9 205.4 %reduce-scatter.9.cloned.1.call-start = ((), (), s32[]{:S(2)}) async-start(), calls=%async_computation.7 | async-start | bytes 278528 | tf_op jit(solution)/shard_map/reduce_scatter | solution.py:75
  338.9 297.4 %reduce-scatter.7.cloned.1.call-start = ((), (), s32[]{:S(2)}) async-start(), calls=%async_computation.6 | async-start | bytes 278528 | tf_op jit(solution)/shard_map/reduce_scatter | solution.py:75
  340.0 390.0 %reduce-scatter.5.cloned.1.call-start = ((), (), s32[]{:S(2)}) async-start(), calls=%async_computation.5 | async-start | bytes 278528 | tf_op jit(solution)/shard_map/reduce_scatter | solution.py:75
Sparse Core Ops, SparseCore 0:
  10.1 243.8 all-gather.1
  338.0 111.4 reduce-scatter.10
  454.7 88.4 reduce-scatter.8
  547.7 88.5 reduce-scatter.6
  641.4 88.4 reduce-scatter.4
where the time goes:
time: 739 us; the launch traced here: 738 us
  waiting for transfers between devices  616 us (83%)
  matrix products  79.2 us (11%)
  other arithmetic  18.6 us (3%)
  between operations  14.1 us (2%)
  local copies, waits for them, and re-layouts  9.72 us (1%)
    reduce_scatter x4, waiting for transfers between devices, body(): lax.psum_scatter(term, 'tensor', scatter_dimension=1, tiled=True)  378 us
    all_gather x1, waiting for transfers between devices, body(): every_state = lax.all_gather(owner_states, 'dp', axis=0, tiled=True)  237 us
    dot_general x4, matrix products, body(): jnp.einsum('bhvk,bhk->bhv', state, queries[:, advance_step, 0:0 + heads],...  39.4 us
    dot_general x4, matrix products, body(): jnp.einsum('bhvk,bhk->bhv', state, key_now, precision=lax.Precision.HIGHEST)  35.9 us
  transfers between devices with their start and end apart: 5, of which 5 were waited for; matrix products, arithmetic and copies ran while one was open for 3% of the time, Pallas kernels for 0%

commit v1 on v0

v1 whole, which is shorter than its diff:
```python
import functools

import jax
import jax.numpy as jnp
from jax import lax
from jax.experimental import pallas as pl
from jax.experimental.pallas import tpu as pltpu
from jax.sharding import PartitionSpec as P

MESH = pl.DeviceIdType.MESH
F32 = jnp.float32
BF16 = jnp.bfloat16
NX, NZ = 4, 8
ROWS, STEPS, DK, DV, HEADS = 32, 4, 128, 128, 2
SAMPLES = 16
TAIL = 32
HEAD = HEADS * DV - TAIL
LAG_X = 3
LAG_T = 3
CHUNKS = 2
CROWS = ROWS * STEPS // CHUNKS
PAIRS = [(s, t) for t in range(STEPS) for s in range(t + 1)]


def split(value):
    high = value.astype(BF16).astype(F32)
    return high, value - high


def kernel(
    own, slot, kq_in, v_in, gate_in, decay_in, rate, bias, gain, weight,
    mixed, final,
    g, kq, kq2, kl, ca, cb, cc, cd, ce, gs, gk, wl, hid, fs,
    part, mine, got1, got2, got3, acc,
    zr, xrp, xrm, xo, zsr, zsl, xsp, xsm, fsp, fsm,
    ar, asd, azr, azsr, azsl, s1, r1, s2, r2, s3, r3, fsem, lsem,
):
    dp = lax.axis_index("dp")
    tn = lax.axis_index("tensor")
    x = dp // NZ
    z = dp % NZ
    xp = (x + 1) % NX
    xm = (x + 3) % NX
    y = tn // 4
    zh = (tn // 2) % 2
    core = tn % 2

    def tensor_of(yy, zz, cc_):
        return (yy * 2 + zz) * 2 + cc_

    def rc(src, dst, ss, rs, xx, zz):
        return pltpu.make_async_remote_copy(
            src_ref=src, dst_ref=dst, send_sem=ss, recv_sem=rs,
            device_id=(xx * NZ + zz, tn), device_id_type=MESH,
        )

    def tc(src, dst, ss, rs, to):
        return pltpu.make_async_remote_copy(
            src_ref=src, dst_ref=dst, send_sem=ss, recv_sem=rs,
            device_id=(dp, to), device_id_type=MESH,
        )

    local = pltpu.make_async_copy(own, g.at[x, z], lsem)
    local.start()

    bar = pltpu.get_barrier_semaphore()

    def sig(d, t):
        pl.semaphore_signal(bar, inc=1, device_id=(d, t), device_id_type=MESH)

    partner = tensor_of(y, zh, 1 - core)
    far = tensor_of(y, 1 - zh, core)
    sig(dp, far)
    sig(dp, tensor_of((y + 2) % 4, zh, core))
    sig(dp, tensor_of((y + 1) % 4, zh, core))
    sig(dp, tensor_of((y + 3) % 4, zh, core))
    sig(xp * NZ + z, tn)
    sig(xm * NZ + z, tn)

    @pl.when(z > 0)
    def _():
        sig(dp - 1, tn)

    @pl.when(z < NZ - 1)
    def _():
        sig(dp + 1, tn)

    sig(dp, partner)
    edge = jnp.logical_or(z == 0, z == NZ - 1)

    @pl.when(edge)
    def _():
        pl.semaphore_wait(bar, 8)

    @pl.when(jnp.logical_not(edge))
    def _():
        pl.semaphore_wait(bar, 9)

    def blk(xx, zp, h):
        return g.at[xx, zp, h, pl.ds(0, HEAD)]

    def z_right(zp, h, src):
        return rc(src, blk(x, zp, h), zsr.at[zp, h], zr.at[zp, h], x, z + 1)

    def z_left(zp, h, src):
        return rc(src, blk(x, zp, h), zsl.at[zp, h], zr.at[zp, h], x, z - 1)

    def x_plus(zp, h, src):
        return rc(src, blk(x, zp, h), xsp.at[zp, h], xrp.at[zp, h], xp, z)

    def x_minus(zp, h, src):
        return rc(src, blk(x, zp, h), xsm.at[zp, h], xrm.at[zp, h], xm, z)

    def f_plus(zp):
        return rc(blk(xm, zp, 0), blk(xm, zp, 0), fsp.at[zp], xo.at[zp, 0], xp, z)

    def f_minus(zp):
        return rc(blk(xp, zp, 1), blk(xp, zp, 1), fsm.at[zp], xo.at[zp, 1], xm, z)

    def tail(xx):
        return g.at[xx, z, :, pl.ds(HEAD, TAIL)]

    def tail_half(xx, h):
        return g.at[xx, z, h, pl.ds(HEAD, TAIL)]

    def t_plus(src):
        return rc(src, tail(x), asd.at[0], ar.at[0], xp, z)

    def t_minus(src):
        return rc(src, tail(x), asd.at[1], ar.at[1], xm, z)

    def tf_plus():
        return rc(tail_half(xm, 0), tail_half(xm, 0), asd.at[2], ar.at[2], xp, z)

    def tf_minus():
        return rc(tail_half(xp, 1), tail_half(xp, 1), asd.at[3], ar.at[3], xm, z)

    def tails(zp):
        return g.at[:, zp, :, pl.ds(HEAD, TAIL)]

    def tz_right(zp):
        return rc(tails(zp), tails(zp), azsr.at[zp], azr.at[zp], x, z + 1)

    def tz_left(zp):
        return rc(tails(zp), tails(zp), azsl.at[zp], azr.at[zp], x, z - 1)

    t_plus(own.at[:, pl.ds(HEAD, TAIL)]).start()
    t_minus(own.at[:, pl.ds(HEAD, TAIL)]).start()
    for h in range(2):
        src = own.at[h, pl.ds(0, HEAD)]

        @pl.when(z < NZ - 1)
        def _():
            z_right(z, h, src).start()

        @pl.when(z > 0)
        def _():
            z_left(z, h, src).start()

        x_plus(z, h, src).start()
        x_minus(z, h, src).start()
    rc(tail(xm), tail(xm), asd.at[0], ar.at[0], xp, z).wait_recv()
    tf_plus().start()
    rc(tail(xp), tail(xp), asd.at[1], ar.at[1], xm, z).wait_recv()
    tf_minus().start()

    def prepare_keys():
        raw = kq_in[...].astype(F32)
        unit = raw * lax.rsqrt(jnp.sum(raw * raw, axis=1, keepdims=True) + 1e-6)
        kind = lax.broadcasted_iota(jnp.int32, unit.shape, 0) % 8
        unit = jnp.where(kind >= STEPS, unit * (DK**-0.5), unit)
        kq[...] = unit
        high, low = split(unit)
        for i in range(2 * STEPS):
            one = kq[pl.ds(i, ROWS, stride=8), :]
            high, low = split(one)
            kq2[pl.ds(i, ROWS, stride=16), :] = high
            kq2[pl.ds(i + 8, ROWS, stride=16), :] = low
            if i < STEPS:
                kl[pl.ds(i, ROWS, stride=16), :] = high
                kl[pl.ds(i + 4, ROWS, stride=16), :] = high
                kl[pl.ds(i + 8, ROWS, stride=16), :] = low
                kl[pl.ds(i + 12, ROWS, stride=16), :] = jnp.zeros_like(low)

    def prepare_gates():
        shape = (ROWS, DV)
        keys = [kq[pl.ds(i, ROWS, stride=8), :] for i in range(2 * STEPS)]
        kk, kqd = {}, {}
        for s, t in PAIRS:
            if s < t:
                kk[s, t] = jnp.sum(keys[s] * keys[t], axis=1, keepdims=True)
            kqd[s, t] = jnp.sum(keys[s] * keys[STEPS + t], axis=1, keepdims=True)
        for h in range(HEADS):
            alpha = []
            for t in range(STEPS):
                d = decay_in[:, pl.ds(t * 4 + h, 1)] + bias[h]
                soft = jnp.maximum(d, 0.0) + jnp.log1p(jnp.exp(-jnp.abs(d)))
                alpha.append(jnp.exp(-rate[h] * soft))
                b = decay_in[:, pl.ds(t * 4 + 2 + h, 1)]
                cb[h, t] = jnp.broadcast_to(1.0 / (1.0 + jnp.exp(-b)), shape)
            for t in range(STEPS):
                run = None
                for s in range(t, -1, -1):
                    n = PAIRS.index((s, t))
                    dot = kqd[s, t]
                    cd[h, n] = jnp.broadcast_to(dot if run is None else run * dot, shape)
                    if s < t:
                        cc[h, n] = jnp.broadcast_to(run * kk[s, t], shape)
                    if t == STEPS - 1:
                        ce[h, s] = jnp.broadcast_to(
                            jnp.ones_like(dot) if run is None else run, shape
                        )
                    run = alpha[s] if run is None else run * alpha[s]
                ca[h, t] = jnp.broadcast_to(run, shape)
                gate = gate_in[:, pl.ds((t * HEADS + h) * DV, DV)].astype(F32)
                gs[h, t] = gain[...] * gate / (1.0 + jnp.exp(-gate))

    def forward(zp):
        rc(blk(xm, zp, 0), blk(xm, zp, 0), fsp.at[zp], xrp.at[zp, 0], xp, z).wait_recv()
        f_plus(zp).start()
        rc(blk(xp, zp, 1), blk(xp, zp, 1), fsm.at[zp], xrm.at[zp, 1], xm, z).wait_recv()
        f_minus(zp).start()

    def gather_step(s, carry):
        zl = z - s
        zg = z + s
        for h in range(2):

            @pl.when(jnp.logical_and(s < NZ, zl >= 0))
            def _():
                z_right(zl, h, blk(x, zl, h)).wait_recv()

                @pl.when(z < NZ - 1)
                def _():
                    z_right(zl, h, blk(x, zl, h)).start()

                x_plus(zl, h, blk(x, zl, h)).start()
                x_minus(zl, h, blk(x, zl, h)).start()

            @pl.when(jnp.logical_and(s < NZ, zg < NZ))
            def _():
                z_left(zg, h, blk(x, zg, h)).wait_recv()

                @pl.when(z > 0)
                def _():
                    z_left(zg, h, blk(x, zg, h)).start()

                x_plus(zg, h, blk(x, zg, h)).start()
                x_minus(zg, h, blk(x, zg, h)).start()

        d = s - LAG_T

        @pl.when(d == 0)
        def _():
            rc(tail_half(x, 0), tail_half(x, 0), asd.at[2], ar.at[2], xp, z).wait_recv()
            rc(tail_half(x, 1), tail_half(x, 1), asd.at[3], ar.at[3], xm, z).wait_recv()
            local.wait()

            @pl.when(z < NZ - 1)
            def _():
                tz_right(z).start()

            @pl.when(z > 0)
            def _():
                tz_left(z).start()

        @pl.when(jnp.logical_and(d >= 1, z - d >= 0))
        def _():
            tz_right(z - d).wait_recv()

            @pl.when(z < NZ - 1)
            def _():
                tz_right(z - d).start()

        @pl.when(jnp.logical_and(d >= 1, z + d < NZ))
        def _():
            tz_left(z + d).wait_recv()

            @pl.when(z > 0)
            def _():
                tz_left(z + d).start()

        e = s - LAG_X

        @pl.when(jnp.logical_and(e >= 0, z - e >= 0))
        def _():
            forward(z - e)

        @pl.when(jnp.logical_and(e >= 1, z + e < NZ))
        def _():
            forward(z + e)

        @pl.when(s == 1)
        def _():
            prepare_keys()

        @pl.when(s == 2)
        def _():
            prepare_gates()

        return carry

    lax.fori_loop(1, NZ + max(LAG_X, LAG_T), gather_step, 0)

    def last_blocks(zp, carry):
        rc(blk(xm, zp, 1), blk(xm, zp, 1), xsp.at[zp, 1], xrp.at[zp, 1], xp, z).wait_recv()
        rc(blk(xp, zp, 0), blk(xp, zp, 0), xsm.at[zp, 0], xrm.at[zp, 0], xm, z).wait_recv()
        f_plus(zp).wait_recv()
        f_minus(zp).wait_recv()
        return carry

    lax.fori_loop(0, NZ, last_blocks, 0)

    contract = (((1,), (1,)), ((), ()))

    def state_of(r):
        p = slot[r] // SAMPLES
        return g[p // (2 * NZ), (p // 2) % NZ, p % 2]

    def recall(r, carry):
        high, low = split(state_of(r))
        both = kq2[pl.ds(pl.multiple_of(r * 16, 16), 16), :].astype(BF16)
        a = lax.dot_general(both, high.astype(BF16), contract, preferred_element_type=F32)
        b = lax.dot_general(both, low.astype(BF16), contract, preferred_element_type=F32)
        total = a[0:8] + a[8:16] + b[0:8]
        at = pl.ds(pl.multiple_of(r * 8, 8), 8)
        gk[0, at, :] = total[:, 0:DV]
        gk[1, at, :] = total[:, DV:]
        return carry

    lax.fori_loop(0, ROWS, recall, 0, unroll=4)

    for h in range(HEADS):
        u = []
        for t in range(STEPS):
            seen = ca[h, t] * gk[h, pl.ds(t, ROWS, stride=8), :]
            out = ca[h, t] * gk[h, pl.ds(STEPS + t, ROWS, stride=8), :]
            for s in range(t):
                seen = seen + cc[h, PAIRS.index((s, t))] * u[s]
            value = v_in[:, pl.ds((t * HEADS + h) * DV, DV)].astype(F32)
            u.append(cb[h, t] * (value - seen))
            for s in range(t + 1):
                out = out + cd[h, PAIRS.index((s, t))] * u[s]
            scale = lax.rsqrt(jnp.mean(out * out, axis=1, keepdims=True) + 1e-6)
            hid[pl.ds(t * ROWS, ROWS), pl.ds(h * DV, DV)] = (out * scale * gs[h, t]).astype(BF16)
        for s in range(STEPS):
            high, low = split(ce[h, s] * u[s])
            wl[h, pl.ds(s, ROWS, stride=16), :] = high
            wl[h, pl.ds(s + 4, ROWS, stride=16), :] = low
            wl[h, pl.ds(s + 8, ROWS, stride=16), :] = high
            wl[h, pl.ds(s + 12, ROWS, stride=16), :] = jnp.zeros_like(high)

    def product(c, yy, zz, cr):
        at = tensor_of(yy, zz, cr) * 128
        return jnp.dot(
            hid[pl.ds(c * CROWS, CROWS), :],
            weight[:, pl.ds(pl.multiple_of(at, 128), 128)],
            preferred_element_type=F32,
        )

    def cross(c, yy):
        return tc(part.at[c, yy], got1.at[c, yy], s1.at[c, yy], r1.at[c, yy], partner)

    def along_y(c, hop):
        yy = (y + hop) % 4
        return tc(
            mine.at[c, yy], got2.at[c, hop - 1], s2.at[c, hop - 1], r2.at[c, hop - 1],
            tensor_of(yy, zh, core),
        )

    def along_z(c):
        return tc(acc.at[c, 1 - zh], got3.at[c], s3.at[c], r3.at[c], far)

    hops = (2, 1, 3, 0)
    for c in range(CHUNKS):
        for hop in hops:
            yy = (y + hop) % 4
            for zz in range(2):
                part[c, yy, zz] = product(c, yy, zz, 1 - core)
            cross(c, yy).start()
    for c in range(CHUNKS):
        for hop in hops:
            yy = (y + hop) % 4
            for zz in range(2):
                mine[c, yy, zz] = product(c, yy, zz, core)
            cross(c, yy).wait_recv()
            mine[c, yy] = mine[c, yy] + got1[c, yy]
            if hop:
                along_y(c, hop).start()

    def finish(r, carry):
        state = state_of(r)
        at = pl.ds(pl.multiple_of(r * 16, 16), 16)
        keys = kl[at, :].astype(BF16)
        for h in range(HEADS):
            update = lax.dot_general(
                wl[h, at, :].astype(BF16), keys, (((0,), (0,)), ((), ())),
                preferred_element_type=F32,
            )
            decay = ca[h, STEPS - 1, pl.ds(r, 1), :]
            fs[r, pl.ds(h * DV, DV), :] = (
                decay * state[h * DV : (h + 1) * DV] + update
            ).astype(BF16)
        return carry

    def write(i):
        part_rows = pl.ds(i * (ROWS // 2), ROWS // 2)
        return pltpu.make_async_copy(fs.at[part_rows], final.at[part_rows], fsem.at[i])

    lax.fori_loop(0, ROWS // 2, finish, 0, unroll=2)
    write(0).start()
    for c in range(CHUNKS):
        for hop in (1, 3, 2):
            along_y(c, hop).wait_recv()
        acc[c] = mine[c, y] + got2[c, 0] + got2[c, 1] + got2[c, 2]
        along_z(c).start()
    lax.fori_loop(ROWS // 2, ROWS, finish, 0, unroll=2)
    write(1).start()
    for c in range(CHUNKS):
        along_z(c).wait_recv()
        done = (acc[c, zh] + got3[c]).astype(BF16)
        for i in range(STEPS // CHUNKS):
            t = c * (STEPS // CHUNKS) + i
            mixed[:, pl.ds(t * 128, 128)] = done[i * ROWS : (i + 1) * ROWS]

    t_plus(tail(x)).wait_send()
    t_minus(tail(x)).wait_send()
    tf_plus().wait_send()
    tf_minus().wait_send()

    def sent(zp, carry):
        for h in range(2):
            x_plus(zp, h, blk(x, zp, h)).wait_send()
            x_minus(zp, h, blk(x, zp, h)).wait_send()

            @pl.when(jnp.logical_and(z < NZ - 1, zp <= z))
            def _():
                z_right(zp, h, blk(x, zp, h)).wait_send()

            @pl.when(jnp.logical_and(z > 0, zp >= z))
            def _():
                z_left(zp, h, blk(x, zp, h)).wait_send()

        @pl.when(jnp.logical_and(z < NZ - 1, zp <= z))
        def _():
            tz_right(zp).wait_send()

        @pl.when(jnp.logical_and(z > 0, zp >= z))
        def _():
            tz_left(zp).wait_send()

        f_plus(zp).wait_send()
        f_minus(zp).wait_send()
        return carry

    lax.fori_loop(0, NZ, sent, 0)
    for c in range(CHUNKS):
        for yy in range(4):
            cross(c, yy).wait_send()
        for hop in (1, 2, 3):
            along_y(c, hop).wait_send()
        along_z(c).wait_send()
    write(0).wait()
    write(1).wait()


def body(
    owner_states, sample_slot, query_in, key_in, value_in, gate_in, decay_in,
    decay_rate, dt_bias, norm_gain, out_weight,
):
    kq = jnp.concatenate([key_in, query_in], axis=1).reshape(ROWS * 8, DK)
    vmem = pl.BlockSpec(memory_space=pltpu.VMEM)
    smem = pl.BlockSpec(memory_space=pltpu.SMEM)
    anywhere = pl.BlockSpec(memory_space=pl.ANY)
    dma = pltpu.SemaphoreType.DMA
    npair = len(PAIRS)
    mixed, final = pl.pallas_call(
        kernel,
        out_shape=(
            jax.ShapeDtypeStruct((ROWS, STEPS * 128), BF16),
            jax.ShapeDtypeStruct((ROWS, HEADS * DV, DK), BF16),
        ),
        in_specs=[anywhere, smem, vmem, vmem, vmem, vmem, smem, smem, vmem, vmem],
        out_specs=(vmem, anywhere),
        scratch_shapes=[
            pltpu.VMEM((NX, NZ, 2, HEADS * DV, DK), F32),
            pltpu.VMEM((ROWS * 8, DK), F32),
            pltpu.VMEM((ROWS * 16, DK), F32),
            pltpu.VMEM((ROWS * 16, DK), F32),
            pltpu.VMEM((HEADS, STEPS, ROWS, DV), F32),
            pltpu.VMEM((HEADS, STEPS, ROWS, DV), F32),
            pltpu.VMEM((HEADS, npair, ROWS, DV), F32),
            pltpu.VMEM((HEADS, npair, ROWS, DV), F32),
            pltpu.VMEM((HEADS, STEPS, ROWS, DV), F32),
            pltpu.VMEM((HEADS, STEPS, ROWS, DV), F32),
            pltpu.VMEM((HEADS, ROWS * 8, DV), F32),
            pltpu.VMEM((HEADS, ROWS * 16, DV), F32),
            pltpu.VMEM((ROWS * STEPS, HEADS * DV), BF16),
            pltpu.VMEM((ROWS, HEADS * DV, DK), BF16),
            pltpu.VMEM((CHUNKS, 4, 2, CROWS, 128), F32),
            pltpu.VMEM((CHUNKS, 4, 2, CROWS, 128), F32),
            pltpu.VMEM((CHUNKS, 4, 2, CROWS, 128), F32),
            pltpu.VMEM((CHUNKS, 3, 2, CROWS, 128), F32),
            pltpu.VMEM((CHUNKS, CROWS, 128), F32),
            pltpu.VMEM((CHUNKS, 2, CROWS, 128), F32),
        ]
        + [dma((NZ, 2)) for _ in range(8)]
        + [dma((NZ,)), dma((NZ,)), dma((4,)), dma((4,)), dma((NZ,)), dma((NZ,)), dma((NZ,))]
        + [dma((CHUNKS, 4)), dma((CHUNKS, 4)), dma((CHUNKS, 3)), dma((CHUNKS, 3))]
        + [dma((CHUNKS,)), dma((CHUNKS,)), dma((2,)), dma],
        compiler_params=pltpu.CompilerParams(
            collective_id=0, has_side_effects=True, vmem_limit_bytes=40 * 2**20
        ),
    )(
        owner_states.reshape(2, HEADS * DV, DK),
        sample_slot,
        kq,
        value_in.reshape(ROWS, STEPS * HEADS * DV),
        gate_in.reshape(ROWS, STEPS * HEADS * DV),
        decay_in.reshape(ROWS, STEPS * 2 * HEADS),
        decay_rate,
        dt_bias,
        norm_gain.reshape(1, DV),
        out_weight,
    )
    return mixed.reshape(ROWS, STEPS, 128), final.reshape(ROWS, HEADS, DV, DK)


def solution(mesh):
    return jax.shard_map(
        body,
        mesh=mesh,
        in_specs=(
            P("dp", "tensor", None, None),
            P("dp"),
            P("dp", None, "tensor"),
            P("dp", None, "tensor"),
            P("dp", None, "tensor"),
            P("dp", None, "tensor"),
            P("dp", None, None, "tensor"),
            P("tensor"),
            P("tensor"),
            P(),
            P("tensor", None),
        ),
        out_specs=(P("dp", None, "tensor"), P("dp", "tensor", None, None)),
        check_vma=False,
    )
```

time: 739 us -> 109 us (0.15)
  waiting for transfers between devices: 616 us -> 0 us
  Pallas kernels: 0 us -> 96.2 us
  matrix products: 79.2 us -> 0 us
  other arithmetic: 18.6 us -> 0.81 us
  between operations: 14.1 us -> 0.66 us
    reduce_scatter x4 -> x0, waiting for transfers between devices: 378 us -> none  [body(): lax.psum_scatter(term, 'tensor', scatter_dimension=1, tiled=True)]
    all_gather x1 -> x0, waiting for transfers between devices: 237 us -> none  [body(): every_state = lax.all_gather(owner_states, 'dp', axis=0, tiled=True)]
    pallas_call x0 -> x1, Pallas kernels: none -> 96.2 us  [body(): pl.pallas_call(kernel, out_shape=(jax.ShapeDtypeStruct((ROWS, STEPS * 128...]
    dot_general x12 -> x0, matrix products: 79.2 us -> none  [the longest x4 39.4 us: body(): jnp.einsum('bhvk,bhk->bhv', state, queries[:, advance_step, 0:0 + heads],...]
    convert_element_type x2 -> x0, other arithmetic: 8.79 us -> none  [the longest x1 8.73 us: body(): return (mixed.astype(jnp.bfloat16), state.astype(jnp.bfloat16))]
  transfers between devices with their start and end apart: 5 -> 0, of which waited for: 5 -> 0; matrix products, arithmetic and copies ran while one was open for 3% -> 0% of each run, Pallas kernels for 0% -> 0%
where the time goes in v1:
time: 109 us; the launch traced here: 107 us
  Pallas kernels  96.2 us (88%)
  local copies, waits for them, and re-layouts  9.21 us (8%)
    pallas_call x1, Pallas kernels, body(): pl.pallas_call(kernel, out_shape=(jax.ShapeDtypeStruct((ROWS, STEPS * 128...  96.2 us
    unnamed x15, local copies, waits for them, and re-layouts  7.81 us

profile of v1, /device:TPU:6, one launch (start us, length us, event | category | flops | bytes accessed | tf_op | source)
XLA Modules:
  0.0 106.8 jit_solution(9246427760676536309)
XLA Ops:
  0.6 0.8 copy.14.decay_in
  1.4 0.8 maximum_bitcast_fusion.kq_in
  2.2 0.9 copy.15
  3.1 0.9 copy.16
  3.9 0.0 copy-start
  3.9 1.2 %copy-done = bf16[256,2048]{1,0:T(8,128)(2,1)S(1)} copy-done((bf16[256,2048]{1,0:T(8,128)(2,1)S(1)}, bf16[256,2048]{1,0:T(8,128)(2,1)}, u32[]{:S(2)}) %copy-start) | copy-done | bytes 1048600
  5.2 0.0 copy-start.1
  5.2 0.9 copy-done.1
  6.1 0.0 copy-start.2
  6.1 0.7 copy-done.2
  6.8 0.0 copy-start.3
  6.8 0.7 copy-done.3
  7.4 0.0 copy-start.4
  7.4 0.7 copy-done.4
  8.1 0.0 copy-start.5
  8.1 0.7 copy-done.5
  8.7 96.2 %shard_map.122 = (bf16[32,512]{1,0:T(8,128)(2,1)S(1)}, bf16[32,256,128]{2,1,0:T(8,128)(2,1)S(1)}) custom-call(f32[2,256,128]{2,1,0:T(8,128)S(1)} %bitcast.13, s32[32]{0:T(128)S(1)} %copy-done.2, bf16[256,128]{1,0:T(8,128)(2,1)S(1)} %maximum_bitcast_fusion.kq_in, bf16[32,1024]{1,0:T(8,128)(2,1)S(1)} %bitcast.11, bf16[32,1024]{1,0:T(8,128)(2,1)S(1)} %bitcast.12, ...), custom_call_target="tpu_custom_call" | custom-call | tf_op jit(solution)/shard_map/pallas_call | solution.py:477
  104.9 0.6 reshape.34
  105.5 1.3 %copy.18 = bf16[32,2,128,128]{3,2,1,0:T(8,128)(2,1)} copy(bf16[32,2,128,128]{3,2,1,0:T(8,128)(2,1)S(1)} %bitcast.10) | data formatting | bytes 4194304
Async XLA Ops:
  3.9 1.2 %copy-start = (bf16[256,2048]{1,0:T(8,128)(2,1)S(1)}, bf16[256,2048]{1,0:T(8,128)(2,1)}, u32[]{:S(2)}) copy-start(bf16[256,2048]{1,0:T(8,128)(2,1)} %weight.1) | copy-start | bytes 3145732
  5.2 0.9 copy-start.1
  6.1 0.7 copy-start.2
  6.8 0.7 copy-start.3
  7.4 0.7 copy-start.4
  8.1 0.7 copy-start.5

commit v2 on v1

--- a/solution.py
+++ b/solution.py
@@ -13,11 +13,12 @@
 NX, NZ = 4, 8
 ROWS, STEPS, DK, DV, HEADS = 32, 4, 128, 128, 2
 SAMPLES = 16
-TAIL = 32
+TAIL = 40
 HEAD = HEADS * DV - TAIL
-LAG_X = 3
+FIRST, APART = 14, 3
 LAG_T = 3
 CHUNKS = 2
+PIECES = 8
 CROWS = ROWS * STEPS // CHUNKS
 PAIRS = [(s, t) for t in range(STEPS) for s in range(t + 1)]
 
@@ -28,12 +29,13 @@
 
 
 def kernel(
-    own, slot, kq_in, v_in, gate_in, decay_in, rate, bias, gain, weight,
+    own, slot_in, q_in, k_in, v_in, gate_in, decay_in, rate_in, bias_in, gain_in, weight_in,
     mixed, final,
-    g, kq, kq2, kl, ca, cb, cc, cd, ce, gs, gk, wl, hid, fs,
-    part, mine, got1, got2, got3, acc,
+    slot, qb, kb, vb, gb, db, rate, bias, gain, weight,
+    g, q32, k32, v32, g32, dt, kq, kq2, kl, ca, cb, cc, cd, ce, gs, gk, wl, hid, fs,
+    part, mine, got1, got2, got3, acc, near, m32,
     zr, xrp, xrm, xo, zsr, zsl, xsp, xsm, fsp, fsm,
-    ar, asd, azr, azsr, azsl, s1, r1, s2, r2, s3, r3, fsem, lsem,
+    ar, asd, azr, azsr, azsl, s1, r1, s2, r2, s3, r3, fsem, lsem, isem,
 ):
     dp = lax.axis_index("dp")
     tn = lax.axis_index("tensor")
@@ -61,7 +63,15 @@
         )
 
     local = pltpu.make_async_copy(own, g.at[x, z], lsem)
-    local.start()
+    inputs = [
+        pltpu.make_async_copy(src, dst, isem.at[i])
+        for i, (src, dst) in enumerate(
+            (
+                (k_in, kb), (q_in, qb), (v_in, vb), (gate_in, gb), (decay_in, db), (rate_in, rate),
+                (bias_in, bias), (gain_in, gain), (slot_in, slot), (weight_in, weight),
+            )
+        )
+    ]
 
     bar = pltpu.get_barrier_semaphore()
 
@@ -159,20 +169,27 @@
 
         x_plus(z, h, src).start()
         x_minus(z, h, src).start()
+    local.start()
+    for copy in inputs:
+        copy.start()
     rc(tail(xm), tail(xm), asd.at[0], ar.at[0], xp, z).wait_recv()
     tf_plus().start()
     rc(tail(xp), tail(xp), asd.at[1], ar.at[1], xm, z).wait_recv()
     tf_minus().start()
 
     def prepare_keys():
-        raw = kq_in[...].astype(F32)
-        unit = raw * lax.rsqrt(jnp.sum(raw * raw, axis=1, keepdims=True) + 1e-6)
-        kind = lax.broadcasted_iota(jnp.int32, unit.shape, 0) % 8
-        unit = jnp.where(kind >= STEPS, unit * (DK**-0.5), unit)
-        kq[...] = unit
-        high, low = split(unit)
+        for copy in inputs:
+            copy.wait()
+        for src, dst in ((kb, k32), (qb, q32), (vb, v32), (gb, g32)):
+            dst[...] = src[...].astype(F32)
+        for n in range(STEPS * 2):
+            dt[pl.ds(2 * n, 2), pl.ds(0, ROWS)] = db[n // 2, n % 2]
         for i in range(2 * STEPS):
-            one = kq[pl.ds(i, ROWS, stride=8), :]
+            raw = k32[:, i, :] if i < STEPS else q32[:, i - STEPS, :]
+            one = raw * lax.rsqrt(jnp.sum(raw * raw, axis=1, keepdims=True) + 1e-6)
+            if i >= STEPS:
+                one = one * (DK**-0.5)
+            kq[i] = one
             high, low = split(one)
             kq2[pl.ds(i, ROWS, stride=16), :] = high
             kq2[pl.ds(i + 8, ROWS, stride=16), :] = low
@@ -184,7 +201,8 @@
 
     def prepare_gates():
         shape = (ROWS, DV)
-        keys = [kq[pl.ds(i, ROWS, stride=8), :] for i in range(2 * STEPS)]
+        scalars = jnp.transpose(dt[...])
+        keys = [kq[i] for i in range(2 * STEPS)]
         kk, kqd = {}, {}
         for s, t in PAIRS:
             if s < t:
@@ -193,10 +211,10 @@
         for h in range(HEADS):
             alpha = []
             for t in range(STEPS):
-                d = decay_in[:, pl.ds(t * 4 + h, 1)] + bias[h]
+                d = scalars[0:ROWS, t * 4 + h : t * 4 + h + 1] + bias[h]
                 soft = jnp.maximum(d, 0.0) + jnp.log1p(jnp.exp(-jnp.abs(d)))
                 alpha.append(jnp.exp(-rate[h] * soft))
-                b = decay_in[:, pl.ds(t * 4 + 2 + h, 1)]
+                b = scalars[0:ROWS, t * 4 + 2 + h : t * 4 + 3 + h]
                 cb[h, t] = jnp.broadcast_to(1.0 / (1.0 + jnp.exp(-b)), shape)
             for t in range(STEPS):
                 run = None
@@ -212,7 +230,7 @@
                         )
                     run = alpha[s] if run is None else run * alpha[s]
                 ca[h, t] = jnp.broadcast_to(run, shape)
-                gate = gate_in[:, pl.ds((t * HEADS + h) * DV, DV)].astype(F32)
+                gate = g32[:, t, pl.ds(h * DV, DV)]
                 gs[h, t] = gain[...] * gate / (1.0 + jnp.exp(-gate))
 
     def forward(zp):
@@ -280,15 +298,18 @@
             def _():
                 tz_left(z + d).start()
 
-        e = s - LAG_X
-
-        @pl.when(jnp.logical_and(e >= 0, z - e >= 0))
-        def _():
-            forward(z - e)
-
-        @pl.when(jnp.logical_and(e >= 1, z + e < NZ))
-        def _():
-            forward(z + e)
+        def onward(r, carry):
+            both = jnp.minimum(z, NZ - 1 - z)
+            paired = r <= 2 * both
+            away = jnp.where(paired, (r + 1) // 2, r - both)
+            below = jnp.where(paired, r % 2 == 1, z >= NZ // 2)
+            forward(jnp.where(below, z - away, z + away))
+            return carry
+
+        def rank_at(quarter):
+            return jnp.clip((quarter - FIRST + APART - 1 + 16 * APART) // APART - 16, 0, NZ)
+
+        lax.fori_loop(rank_at(4 * s), rank_at(4 * s + 4), onward, 0)
 
         @pl.when(s == 1)
         def _():
@@ -300,7 +321,7 @@
 
         return carry
 
-    lax.fori_loop(1, NZ + max(LAG_X, LAG_T), gather_step, 0)
+    lax.fori_loop(1, max(NZ + LAG_T, (FIRST + (NZ - 1) * APART) // 4 + 1), gather_step, 0)
 
     def last_blocks(zp, carry):
         rc(blk(xm, zp, 1), blk(xm, zp, 1), xsp.at[zp, 1], xrp.at[zp, 1], xp, z).wait_recv()
@@ -328,65 +349,89 @@
         gk[1, at, :] = total[:, DV:]
         return carry
 
-    lax.fori_loop(0, ROWS, recall, 0, unroll=4)
-
-    for h in range(HEADS):
+    lax.fori_loop(0, ROWS, recall, 0, unroll=8)
+
+    def run_steps(h, carry):
+        lanes = pl.ds(pl.multiple_of(h * DV, DV), DV)
         u = []
         for t in range(STEPS):
             seen = ca[h, t] * gk[h, pl.ds(t, ROWS, stride=8), :]
             out = ca[h, t] * gk[h, pl.ds(STEPS + t, ROWS, stride=8), :]
             for s in range(t):
                 seen = seen + cc[h, PAIRS.index((s, t))] * u[s]
-            value = v_in[:, pl.ds((t * HEADS + h) * DV, DV)].astype(F32)
+            value = v32[:, t, lanes]
             u.append(cb[h, t] * (value - seen))
             for s in range(t + 1):
                 out = out + cd[h, PAIRS.index((s, t))] * u[s]
             scale = lax.rsqrt(jnp.mean(out * out, axis=1, keepdims=True) + 1e-6)
-            hid[pl.ds(t * ROWS, ROWS), pl.ds(h * DV, DV)] = (out * scale * gs[h, t]).astype(BF16)
+            hid[pl.ds(t * ROWS, ROWS), lanes] = (out * scale * gs[h, t]).astype(BF16)
         for s in range(STEPS):
             high, low = split(ce[h, s] * u[s])
             wl[h, pl.ds(s, ROWS, stride=16), :] = high
             wl[h, pl.ds(s + 4, ROWS, stride=16), :] = low
             wl[h, pl.ds(s + 8, ROWS, stride=16), :] = high
             wl[h, pl.ds(s + 12, ROWS, stride=16), :] = jnp.zeros_like(high)
-
-    def product(c, yy, zz, cr):
-        at = tensor_of(yy, zz, cr) * 128
-        return jnp.dot(
-            hid[pl.ds(c * CROWS, CROWS), :],
-            weight[:, pl.ds(pl.multiple_of(at, 128), 128)],
-            preferred_element_type=F32,
+        return carry
+
+    lax.fori_loop(0, HEADS, run_steps, 0)
+
+    def cross(side, c, yy):
+        at = (side, c, yy)
+        return tc(part.at[at], got1.at[at], s1.at[at], r1.at[at], partner)
+
+    def along_y(side, c, hop):
+        at = (side, c, hop - 1)
+        return tc(
+            mine.at[side, c, (y + hop) % 4], got2.at[at], s2.at[at], r2.at[at],
+            tensor_of((y + hop) % 4, zh, core),
         )
 
-    def cross(c, yy):
-        return tc(part.at[c, yy], got1.at[c, yy], s1.at[c, yy], r1.at[c, yy], partner)
-
-    def along_y(c, hop):
+    def along_z(c):
+        return tc(acc.at[c], got3.at[c], s3.at[c], r3.at[c], far)
+
+    def product(n, carry):
+        side = n // 4
+        yy = (y + 1 + n) % 4
+        zz = (zh + 1 + side) % 2
+        at = pl.multiple_of((yy * 2 + zz) * 256, 256)
+        both = jnp.dot(hid[...], weight[:, pl.ds(at, 256)], preferred_element_type=F32)
+        theirs = jnp.where(core == 0, both[:, 128:], both[:, :128])
+        ours = jnp.where(core == 0, both[:, :128], both[:, 128:])
+        for c in range(CHUNKS):
+            part[side, c, yy] = theirs[c * CROWS : (c + 1) * CROWS]
+            mine[side, c, yy] = ours[c * CROWS : (c + 1) * CROWS]
+            cross(side, c, yy).start()
+        return carry
+
+    lax.fori_loop(0, 8, product, 0)
+
+    def merge(n, carry):
+        side = n // (4 * CHUNKS)
+        c = (n // 4) % CHUNKS
+        hop = (n + 1) % 4
         yy = (y + hop) % 4
-        return tc(
-            mine.at[c, yy], got2.at[c, hop - 1], s2.at[c, hop - 1], r2.at[c, hop - 1],
-            tensor_of(yy, zh, core),
-        )
-
-    def along_z(c):
-        return tc(acc.at[c, 1 - zh], got3.at[c], s3.at[c], r3.at[c], far)
-
-    hops = (2, 1, 3, 0)
-    for c in range(CHUNKS):
-        for hop in hops:
-            yy = (y + hop) % 4
-            for zz in range(2):
-                part[c, yy, zz] = product(c, yy, zz, 1 - core)
-            cross(c, yy).start()
-    for c in range(CHUNKS):
-        for hop in hops:
-            yy = (y + hop) % 4
-            for zz in range(2):
-                mine[c, yy, zz] = product(c, yy, zz, core)
-            cross(c, yy).wait_recv()
-            mine[c, yy] = mine[c, yy] + got1[c, yy]
-            if hop:
-                along_y(c, hop).start()
+        cross(side, c, yy).wait_recv()
+        mine[side, c, yy] = mine[side, c, yy] + got1[side, c, yy]
+
+        @pl.when(hop > 0)
+        def _():
+            along_y(side, c, hop).start()
+
+        return carry
+
+    lax.fori_loop(0, 8 * CHUNKS, merge, 0)
+
+    def summed(side, c):
+        for hop in (1, 2, 3):
+            along_y(side, c, hop).wait_recv()
+        return mine[side, c, y] + got2[side, c, 0] + got2[side, c, 1] + got2[side, c, 2]
+
+    def send_z(c, carry):
+        acc[c] = summed(0, c)
+        along_z(c).start()
+        return carry
+
+    lax.fori_loop(0, CHUNKS, send_z, 0)
 
     def finish(r, carry):
         state = state_of(r)
@@ -404,24 +449,15 @@
         return carry
 
     def write(i):
-        part_rows = pl.ds(i * (ROWS // 2), ROWS // 2)
-        return pltpu.make_async_copy(fs.at[part_rows], final.at[part_rows], fsem.at[i])
-
-    lax.fori_loop(0, ROWS // 2, finish, 0, unroll=2)
-    write(0).start()
-    for c in range(CHUNKS):
-        for hop in (1, 3, 2):
-            along_y(c, hop).wait_recv()
-        acc[c] = mine[c, y] + got2[c, 0] + got2[c, 1] + got2[c, 2]
-        along_z(c).start()
-    lax.fori_loop(ROWS // 2, ROWS, finish, 0, unroll=2)
-    write(1).start()
-    for c in range(CHUNKS):
-        along_z(c).wait_recv()
-        done = (acc[c, zh] + got3[c]).astype(BF16)
-        for i in range(STEPS // CHUNKS):
-            t = c * (STEPS // CHUNKS) + i
-            mixed[:, pl.ds(t * 128, 128)] = done[i * ROWS : (i + 1) * ROWS]
+        some = pl.ds(i * (ROWS // 2), ROWS // 2)
+        return pltpu.make_async_copy(fs.at[some], final.at[some], fsem.at[i])
+
+    def half(i, carry):
+        lax.fori_loop(i * (ROWS // 2), (i + 1) * (ROWS // 2), finish, 0)
+        write(i).start()
+        return carry
+
+    lax.fori_loop(0, 2, half, 0)
 
     t_plus(tail(x)).wait_send()
     t_minus(tail(x)).wait_send()
@@ -454,37 +490,91 @@
         return carry
 
     lax.fori_loop(0, NZ, sent, 0)
+
+    def left(n, carry):
+        for yy in range(4):
+            cross(n // CHUNKS, n % CHUNKS, yy).wait_send()
+        for hop in (1, 2, 3):
+            along_y(n // CHUNKS, n % CHUNKS, hop).wait_send()
+        return carry
+
+    lax.fori_loop(0, 2 * CHUNKS, left, 0)
+
+    def keep(c, carry):
+        near[c] = summed(1, c)
+        return carry
+
+    lax.fori_loop(0, CHUNKS, keep, 0)
+
+    def gather_z(c, carry):
+        along_z(c).wait_recv()
+        for i in range(STEPS // CHUNKS):
+            some = pl.ds(i * ROWS, ROWS)
+            m32[:, c * (STEPS // CHUNKS) + i, :] = near[c, some] + got3[c, some]
+        return carry
+
+    lax.fori_loop(0, CHUNKS, gather_z, 0)
+    mixed[...] = m32[...].astype(BF16)
+
     for c in range(CHUNKS):
-        for yy in range(4):
-            cross(c, yy).wait_send()
-        for hop in (1, 2, 3):
-            along_y(c, hop).wait_send()
         along_z(c).wait_send()
     write(0).wait()
     write(1).wait()
+
+
+def hand_over(mixed_in, final_in, mixed, final, held, kept, sem):
+    size = ROWS // PIECES
+    pieces = [pl.ds(i * size, size) for i in range(PIECES)]
+    reads = [pltpu.make_async_copy(final_in.at[p], held.at[p], sem.at[i]) for i, p in enumerate(pieces)]
+    reads.append(pltpu.make_async_copy(mixed_in, kept, sem.at[PIECES]))
+    writes = [
+        pltpu.make_async_copy(held.at[p], final.at[p], sem.at[PIECES + 1 + i])
+        for i, p in enumerate(pieces)
+    ]
+    writes.append(pltpu.make_async_copy(kept, mixed, sem.at[2 * PIECES + 1]))
+    for read in reads:
+        read.start()
+    for read, write in zip(reads, writes):
+        read.wait()
+        write.start()
+    for write in writes:
+        write.wait()
 
 
 def body(
     owner_states, sample_slot, query_in, key_in, value_in, gate_in, decay_in,
     decay_rate, dt_bias, norm_gain, out_weight,
 ):
-    kq = jnp.concatenate([key_in, query_in], axis=1).reshape(ROWS * 8, DK)
     vmem = pl.BlockSpec(memory_space=pltpu.VMEM)
-    smem = pl.BlockSpec(memory_space=pltpu.SMEM)
-    anywhere = pl.BlockSpec(memory_space=pl.ANY)
+    hbm = pl.BlockSpec(memory_space=pltpu.HBM)
     dma = pltpu.SemaphoreType.DMA
     npair = len(PAIRS)
     mixed, final = pl.pallas_call(
         kernel,
         out_shape=(
-            jax.ShapeDtypeStruct((ROWS, STEPS * 128), BF16),
+            jax.ShapeDtypeStruct((ROWS, STEPS, 128), BF16),
             jax.ShapeDtypeStruct((ROWS, HEADS * DV, DK), BF16),
         ),
-        in_specs=[anywhere, smem, vmem, vmem, vmem, vmem, smem, smem, vmem, vmem],
-        out_specs=(vmem, anywhere),
+        in_specs=[hbm] * 11,
+        out_specs=(vmem, hbm),
         scratch_shapes=[
+            pltpu.SMEM((ROWS,), jnp.int32),
+            pltpu.VMEM((ROWS, STEPS, DK), BF16),
+            pltpu.VMEM((ROWS, STEPS, DK), BF16),
+            pltpu.VMEM((ROWS, STEPS, HEADS * DV), BF16),
+            pltpu.VMEM((ROWS, STEPS, HEADS * DV), BF16),
+            pltpu.VMEM((STEPS, 2, HEADS, ROWS), F32),
+            pltpu.SMEM((HEADS,), F32),
+            pltpu.SMEM((HEADS,), F32),
+            pltpu.VMEM((1, DV), F32),
+            pltpu.VMEM((HEADS * DV, 2048), BF16),
             pltpu.VMEM((NX, NZ, 2, HEADS * DV, DK), F32),
-            pltpu.VMEM((ROWS * 8, DK), F32),
+            pltpu.VMEM((ROWS, STEPS, DK), F32),
+            pltpu.VMEM((ROWS, STEPS, DK), F32),
+            pltpu.VMEM((ROWS, STEPS, HEADS * DV), F32),
+            pltpu.VMEM((ROWS, STEPS, HEADS * DV), F32),
+            pltpu.VMEM((STEPS * 2 * HEADS, 128), F32),
+            pltpu.VMEM((2 * STEPS, ROWS, DK), F32),
             pltpu.VMEM((ROWS * 16, DK), F32),
             pltpu.VMEM((ROWS * 16, DK), F32),
             pltpu.VMEM((HEADS, STEPS, ROWS, DV), F32),
@@ -497,33 +587,51 @@
             pltpu.VMEM((HEADS, ROWS * 16, DV), F32),
             pltpu.VMEM((ROWS * STEPS, HEADS * DV), BF16),
             pltpu.VMEM((ROWS, HEADS * DV, DK), BF16),
-            pltpu.VMEM((CHUNKS, 4, 2, CROWS, 128), F32),
-            pltpu.VMEM((CHUNKS, 4, 2, CROWS, 128), F32),
-            pltpu.VMEM((CHUNKS, 4, 2, CROWS, 128), F32),
-            pltpu.VMEM((CHUNKS, 3, 2, CROWS, 128), F32),
+            pltpu.VMEM((2, CHUNKS, 4, CROWS, 128), F32),
+            pltpu.VMEM((2, CHUNKS, 4, CROWS, 128), F32),
+            pltpu.VMEM((2, CHUNKS, 4, CROWS, 128), F32),
+            pltpu.VMEM((2, CHUNKS, 3, CROWS, 128), F32),
             pltpu.VMEM((CHUNKS, CROWS, 128), F32),
-            pltpu.VMEM((CHUNKS, 2, CROWS, 128), F32),
+            pltpu.VMEM((CHUNKS, CROWS, 128), F32),
+            pltpu.VMEM((CHUNKS, CROWS, 128), F32),
+            pltpu.VMEM((ROWS, STEPS, 128), F32),
         ]
         + [dma((NZ, 2)) for _ in range(8)]
         + [dma((NZ,)), dma((NZ,)), dma((4,)), dma((4,)), dma((NZ,)), dma((NZ,)), dma((NZ,))]
-        + [dma((CHUNKS, 4)), dma((CHUNKS, 4)), dma((CHUNKS, 3)), dma((CHUNKS, 3))]
-        + [dma((CHUNKS,)), dma((CHUNKS,)), dma((2,)), dma],
+        + [dma((2, CHUNKS, 4)), dma((2, CHUNKS, 4)), dma((2, CHUNKS, 3)), dma((2, CHUNKS, 3))]
+        + [dma((CHUNKS,)), dma((CHUNKS,)), dma((2,)), dma, dma((10,))],
         compiler_params=pltpu.CompilerParams(
-            collective_id=0, has_side_effects=True, vmem_limit_bytes=40 * 2**20
+            collective_id=0, has_side_effects=True, vmem_limit_bytes=56 * 2**20
         ),
     )(
         owner_states.reshape(2, HEADS * DV, DK),
         sample_slot,
-        kq,
-        value_in.reshape(ROWS, STEPS * HEADS * DV),
-        gate_in.reshape(ROWS, STEPS * HEADS * DV),
-        decay_in.reshape(ROWS, STEPS * 2 * HEADS),
+        query_in,
+        key_in,
+        value_in,
+        gate_in,
+        decay_in.transpose(1, 2, 3, 0),
         decay_rate,
         dt_bias,
         norm_gain.reshape(1, DV),
         out_weight,
     )
-    return mixed.reshape(ROWS, STEPS, 128), final.reshape(ROWS, HEADS, DV, DK)
+    mixed, final = pl.pallas_call(
+        hand_over,
+        out_shape=(
+            jax.ShapeDtypeStruct((ROWS, STEPS, 128), BF16),
+            jax.ShapeDtypeStruct((ROWS, HEADS * DV, DK), BF16),
+        ),
+        in_specs=[hbm, hbm],
+        out_specs=(hbm, hbm),
+        scratch_shapes=[
+            pltpu.VMEM((ROWS, HEADS * DV, DK), BF16),
+            pltpu.VMEM((ROWS, STEPS, 128), BF16),
+            dma((2 * PIECES + 2,)),
+        ],
+        compiler_params=pltpu.CompilerParams(vmem_limit_bytes=56 * 2**20),
+    )(mixed, final)
+    return mixed, final.reshape(ROWS, HEADS, DV, DK)
 
 
 def solution(mesh):

time: 109 us -> 100 us (0.917)
  local copies, waits for them, and re-layouts: 9.21 us -> 0 us
  Pallas kernels: 96.2 us -> 98.2 us
    unnamed x15 -> x0, local copies, waits for them, and re-layouts: 7.81 us -> none
    pallas_call x1 -> x2, Pallas kernels: 96.2 us -> 98.2 us  [the longest x1 95.8 us: body(): pl.pallas_call(kernel, out_shape=(jax.ShapeDtypeStruct((ROWS, STEPS, 128)...]
    reshape x2 -> x0, local copies, waits for them, and re-layouts: 1.4 us -> none  [the longest x1 0.77 us: body(): decay_in.reshape(ROWS, STEPS * 2 * HEADS)]
where the time goes in v2:
time: 100 us; the launch traced here: 98.8 us
  Pallas kernels  98.2 us (98%)
    pallas_call x1, Pallas kernels, body(): pl.pallas_call(kernel, out_shape=(jax.ShapeDtypeStruct((ROWS, STEPS, 128)...  95.8 us
    pallas_call x1, Pallas kernels, body(): pl.pallas_call(hand_over, out_shape=(jax.ShapeDtypeStruct((ROWS, STEPS, 1...  2.42 us

profile of v2, /device:TPU:6, one launch (start us, length us, event | category | flops | bytes accessed | tf_op | source)
XLA Modules:
  0.0 98.8 jit_solution(17631151244436401965)
XLA Ops:
  0.6 95.8 %shard_map.122 = (bf16[32,4,128]{2,1,0:T(4,128)(2,1)}, bf16[32,256,128]{2,1,0:T(8,128)(2,1)}) custom-call(f32[2,256,128]{2,1,0:T(8,128)} %bitcast.4, s32[32]{0:T(128)} %slot_in.1, bf16[32,4,128]{2,1,0:T(4,128)(2,1)} %q_in.1, bf16[32,4,128]{2,1,0:T(4,128)(2,1)} %k_in.1, bf16[32,4,256]{2,1,0:T(4,128)(2,1)} %v_in.1, bf16[32,4,256]{2,1,0:T(4,128)(2,1)} %gate_in.1, ...), custom_call_target="tpu_custom_call" | custom-call | tf_op jit(solution)/shard_map/pallas_call | solution.py:552
  96.4 2.4 %shard_map.123 = (bf16[32,4,128]{2,1,0:T(4,128)(2,1)}, bf16[32,256,128]{2,1,0:T(8,128)(2,1)}) custom-call(bf16[32,4,128]{2,1,0:T(4,128)(2,1)} %get-tuple-element.6.mixed_in, bf16[32,256,128]{2,1,0:T(8,128)(2,1)} %get-tuple-element.7.final_in), custom_call_target="tpu_custom_call" | custom-call | tf_op jit(solution)/shard_map/pallas_call | solution.py:619

commit v3 on v2

--- a/solution.py
+++ b/solution.py
@@ -18,7 +18,7 @@
 FIRST, APART = 14, 3
 LAG_T = 3
 CHUNKS = 2
-PIECES = 8
+PIECES = 4
 CROWS = ROWS * STEPS // CHUNKS
 PAIRS = [(s, t) for t in range(STEPS) for s in range(t + 1)]
 
@@ -32,10 +32,10 @@
     own, slot_in, q_in, k_in, v_in, gate_in, decay_in, rate_in, bias_in, gain_in, weight_in,
     mixed, final,
     slot, qb, kb, vb, gb, db, rate, bias, gain, weight,
-    g, q32, k32, v32, g32, dt, kq, kq2, kl, ca, cb, cc, cd, ce, gs, gk, wl, hid, fs,
+    g, q32, k32, v32, g32, dt, kq, kq2, kl, ca, cb, cc, cd, ce, gs, gk, wl, hid,
     part, mine, got1, got2, got3, acc, near, m32,
     zr, xrp, xrm, xo, zsr, zsl, xsp, xsm, fsp, fsm,
-    ar, asd, azr, azsr, azsl, s1, r1, s2, r2, s3, r3, fsem, lsem, isem,
+    ar, asd, azr, azsr, azsl, s1, r1, s2, r2, s3, r3, lsem, isem, far_in,
 ):
     dp = lax.axis_index("dp")
     tn = lax.axis_index("tensor")
@@ -80,7 +80,11 @@
 
     partner = tensor_of(y, zh, 1 - core)
     far = tensor_of(y, 1 - zh, core)
-    sig(dp, far)
+
+    @pl.when(zh == 0)
+    def _():
+        sig(dp, far)
+
     sig(dp, tensor_of((y + 2) % 4, zh, core))
     sig(dp, tensor_of((y + 1) % 4, zh, core))
     sig(dp, tensor_of((y + 3) % 4, zh, core))
@@ -98,13 +102,21 @@
     sig(dp, partner)
     edge = jnp.logical_or(z == 0, z == NZ - 1)
 
-    @pl.when(edge)
+    @pl.when(jnp.logical_and(edge, zh == 0))
+    def _():
+        pl.semaphore_wait(bar, 7)
+
+    @pl.when(jnp.logical_xor(edge, zh == 0))
     def _():
         pl.semaphore_wait(bar, 8)
 
-    @pl.when(jnp.logical_not(edge))
+    @pl.when(jnp.logical_and(jnp.logical_not(edge), zh == 1))
     def _():
         pl.semaphore_wait(bar, 9)
+
+    @pl.when(zh == 1)
+    def _():
+        pl.semaphore_signal(far_in, inc=1, device_id=(dp, far), device_id_type=MESH)
 
     def blk(xx, zp, h):
         return g.at[xx, zp, h, pl.ds(0, HEAD)]
@@ -426,6 +438,10 @@
             along_y(side, c, hop).wait_recv()
         return mine[side, c, y] + got2[side, c, 0] + got2[side, c, 1] + got2[side, c, 2]
 
+    @pl.when(zh == 0)
+    def _():
+        pl.semaphore_wait(far_in, 1)
+
     def send_z(c, carry):
         acc[c] = summed(0, c)
         along_z(c).start()
@@ -443,21 +459,12 @@
                 preferred_element_type=F32,
             )
             decay = ca[h, STEPS - 1, pl.ds(r, 1), :]
-            fs[r, pl.ds(h * DV, DV), :] = (
+            final[r, pl.ds(h * DV, DV), :] = (
                 decay * state[h * DV : (h + 1) * DV] + update
             ).astype(BF16)
         return carry
 
-    def write(i):
-        some = pl.ds(i * (ROWS // 2), ROWS // 2)
-        return pltpu.make_async_copy(fs.at[some], final.at[some], fsem.at[i])
-
-    def half(i, carry):
-        lax.fori_loop(i * (ROWS // 2), (i + 1) * (ROWS // 2), finish, 0)
-        write(i).start()
-        return carry
-
-    lax.fori_loop(0, 2, half, 0)
+    lax.fori_loop(0, ROWS, finish, 0)
 
     t_plus(tail(x)).wait_send()
     t_minus(tail(x)).wait_send()
@@ -518,27 +525,19 @@
 
     for c in range(CHUNKS):
         along_z(c).wait_send()
-    write(0).wait()
-    write(1).wait()
-
-
-def hand_over(mixed_in, final_in, mixed, final, held, kept, sem):
+
+
+def hand_over(mixed_in, final_in, mixed, final, sem):
     size = ROWS // PIECES
-    pieces = [pl.ds(i * size, size) for i in range(PIECES)]
-    reads = [pltpu.make_async_copy(final_in.at[p], held.at[p], sem.at[i]) for i, p in enumerate(pieces)]
-    reads.append(pltpu.make_async_copy(mixed_in, kept, sem.at[PIECES]))
-    writes = [
-        pltpu.make_async_copy(held.at[p], final.at[p], sem.at[PIECES + 1 + i])
-        for i, p in enumerate(pieces)
+    copies = [
+        pltpu.make_async_copy(final_in.at[pl.ds(i * size, size)], final.at[pl.ds(i * size, size)], sem.at[i])
+        for i in range(PIECES)
     ]
-    writes.append(pltpu.make_async_copy(kept, mixed, sem.at[2 * PIECES + 1]))
-    for read in reads:
-        read.start()
-    for read, write in zip(reads, writes):
-        read.wait()
-        write.start()
-    for write in writes:
-        write.wait()
+    copies.append(pltpu.make_async_copy(mixed_in, mixed, sem.at[PIECES]))
+    for copy in copies:
+        copy.start()
+    for copy in copies:
+        copy.wait()
 
 
 def body(
@@ -549,14 +548,30 @@
     hbm = pl.BlockSpec(memory_space=pltpu.HBM)
     dma = pltpu.SemaphoreType.DMA
     npair = len(PAIRS)
+    operands = [
+        pltpu.with_memory_space_constraint(value, pltpu.HBM)
+        for value in (
+            owner_states.reshape(2, HEADS * DV, DK),
+            sample_slot,
+            query_in,
+            key_in,
+            value_in,
+            gate_in,
+            decay_in.transpose(1, 2, 3, 0),
+            decay_rate,
+            dt_bias,
+            norm_gain.reshape(1, DV),
+            out_weight,
+        )
+    ]
     mixed, final = pl.pallas_call(
         kernel,
         out_shape=(
-            jax.ShapeDtypeStruct((ROWS, STEPS, 128), BF16),
-            jax.ShapeDtypeStruct((ROWS, HEADS * DV, DK), BF16),
+            pltpu.VMEM((ROWS, STEPS, 128), BF16),
+            pltpu.VMEM((ROWS, HEADS * DV, DK), BF16),
         ),
         in_specs=[hbm] * 11,
-        out_specs=(vmem, hbm),
+        out_specs=(vmem, vmem),
         scratch_shapes=[
             pltpu.SMEM((ROWS,), jnp.int32),
             pltpu.VMEM((ROWS, STEPS, DK), BF16),
@@ -586,7 +601,6 @@
             pltpu.VMEM((HEADS, ROWS * 8, DV), F32),
             pltpu.VMEM((HEADS, ROWS * 16, DV), F32),
             pltpu.VMEM((ROWS * STEPS, HEADS * DV), BF16),
-            pltpu.VMEM((ROWS, HEADS * DV, DK), BF16),
             pltpu.VMEM((2, CHUNKS, 4, CROWS, 128), F32),
             pltpu.VMEM((2, CHUNKS, 4, CROWS, 128), F32),
             pltpu.VMEM((2, CHUNKS, 4, CROWS, 128), F32),
@@ -599,37 +613,21 @@
         + [dma((NZ, 2)) for _ in range(8)]
         + [dma((NZ,)), dma((NZ,)), dma((4,)), dma((4,)), dma((NZ,)), dma((NZ,)), dma((NZ,))]
         + [dma((2, CHUNKS, 4)), dma((2, CHUNKS, 4)), dma((2, CHUNKS, 3)), dma((2, CHUNKS, 3))]
-        + [dma((CHUNKS,)), dma((CHUNKS,)), dma((2,)), dma, dma((10,))],
+        + [dma((CHUNKS,)), dma((CHUNKS,)), dma, dma((10,)), pltpu.SemaphoreType.REGULAR],
         compiler_params=pltpu.CompilerParams(
-            collective_id=0, has_side_effects=True, vmem_limit_bytes=56 * 2**20
+            collective_id=0, has_side_effects=True, vmem_limit_bytes=32 * 2**20
         ),
-    )(
-        owner_states.reshape(2, HEADS * DV, DK),
-        sample_slot,
-        query_in,
-        key_in,
-        value_in,
-        gate_in,
-        decay_in.transpose(1, 2, 3, 0),
-        decay_rate,
-        dt_bias,
-        norm_gain.reshape(1, DV),
-        out_weight,
-    )
+    )(*operands)
     mixed, final = pl.pallas_call(
         hand_over,
         out_shape=(
             jax.ShapeDtypeStruct((ROWS, STEPS, 128), BF16),
             jax.ShapeDtypeStruct((ROWS, HEADS * DV, DK), BF16),
         ),
-        in_specs=[hbm, hbm],
+        in_specs=[vmem, vmem],
         out_specs=(hbm, hbm),
-        scratch_shapes=[
-            pltpu.VMEM((ROWS, HEADS * DV, DK), BF16),
-            pltpu.VMEM((ROWS, STEPS, 128), BF16),
-            dma((2 * PIECES + 2,)),
-        ],
-        compiler_params=pltpu.CompilerParams(vmem_limit_bytes=56 * 2**20),
+        scratch_shapes=[dma((PIECES + 1,))],
+        compiler_params=pltpu.CompilerParams(vmem_limit_bytes=32 * 2**20),
     )(mixed, final)
     return mixed, final.reshape(ROWS, HEADS, DV, DK)
 

time: 100 us -> 95.6 us (0.956)
  Pallas kernels: 98.2 us -> 93.2 us
    pallas_call x1, Pallas kernels: 95.8 us -> 91.9 us  [body(): pl.pallas_call(kernel, out_shape=(pltpu.VMEM((ROWS, STEPS, 128), BF16), p...]
    pallas_call x1, Pallas kernels: 2.42 us -> 1.36 us  [body(): pl.pallas_call(hand_over, out_shape=(jax.ShapeDtypeStruct((ROWS, STEPS, 1...]
where the time goes in v3:
time: 95.6 us; the launch traced here: 93.9 us
  Pallas kernels  93.2 us (97%)
    pallas_call x1, Pallas kernels, body(): pl.pallas_call(kernel, out_shape=(pltpu.VMEM((ROWS, STEPS, 128), BF16), p...  91.9 us

profile of v3, /device:TPU:6, one launch (start us, length us, event | category | flops | bytes accessed | tf_op | source)
XLA Modules:
  0.0 93.9 jit_solution(15328753319982358158)
XLA Ops:
  0.6 91.9 %shard_map.122 = (bf16[32,4,128]{2,1,0:T(4,128)(2,1)S(1)}, bf16[32,256,128]{2,1,0:T(8,128)(2,1)S(1)}) custom-call(f32[2,256,128]{2,1,0:T(8,128)} %bitcast.4, s32[32]{0:T(128)} %slot_in.1, bf16[32,4,128]{2,1,0:T(4,128)(2,1)} %q_in.1, bf16[32,4,128]{2,1,0:T(4,128)(2,1)} %k_in.1, bf16[32,4,256]{2,1,0:T(4,128)(2,1)} %v_in.1, bf16[32,4,256]{2,1,0:T(4,128)(2,1)} %gate_in.1, ...), custom_call_target="tpu_custom_call" | custom-call | tf_op jit(solution)/shard_map/pallas_call | solution.py:567
  92.5 1.4 %shard_map.123 = (bf16[32,4,128]{2,1,0:T(4,128)(2,1)}, bf16[32,256,128]{2,1,0:T(8,128)(2,1)}) custom-call(bf16[32,4,128]{2,1,0:T(4,128)(2,1)S(1)} %get-tuple-element.6.mixed_in, bf16[32,256,128]{2,1,0:T(8,128)(2,1)S(1)} %get-tuple-element.7.final_in), custom_call_target="tpu_custom_call" | custom-call | tf_op jit(solution)/shard_map/pallas_call | solution.py:621

commit v4 on v3

--- a/solution.py
+++ b/solution.py
@@ -32,10 +32,10 @@
     own, slot_in, q_in, k_in, v_in, gate_in, decay_in, rate_in, bias_in, gain_in, weight_in,
     mixed, final,
     slot, qb, kb, vb, gb, db, rate, bias, gain, weight,
-    g, q32, k32, v32, g32, dt, kq, kq2, kl, ca, cb, cc, cd, ce, gs, gk, wl, hid,
-    part, mine, got1, got2, got3, acc, near, m32,
+    g, q32, k32, v32, g32, dt, kq, kq2, kq3, kl, ca, cb, cc, cd, ce, gs, gk, wl, hid,
+    wout, wgot, wall, hout, hgot, mine, got2, got3, acc, near, m32,
     zr, xrp, xrm, xo, zsr, zsl, xsp, xsm, fsp, fsm,
-    ar, asd, azr, azsr, azsl, s1, r1, s2, r2, s3, r3, lsem, isem, far_in,
+    ar, asd, azr, azsr, azsl, wsem, s1, r1, s2, r2, s3, r3, lsem, isem, far_in,
 ):
     dp = lax.axis_index("dp")
     tn = lax.axis_index("tensor")
@@ -188,6 +188,9 @@
     tf_plus().start()
     rc(tail(xp), tail(xp), asd.at[1], ar.at[1], xm, z).wait_recv()
     tf_minus().start()
+
+    def keys_in(i, part, value):
+        kq3[part, pl.ds(i, ROWS, stride=16), :] = value
 
     def prepare_keys():
         for copy in inputs:
@@ -203,13 +206,18 @@
                 one = one * (DK**-0.5)
             kq[i] = one
             high, low = split(one)
-            kq2[pl.ds(i, ROWS, stride=16), :] = high
-            kq2[pl.ds(i + 8, ROWS, stride=16), :] = low
+            keys_in(i, 0, high)
+            keys_in(i, 1, high)
+            keys_in(i + 8, 0, low)
+            keys_in(i + 8, 1, jnp.zeros_like(low))
             if i < STEPS:
                 kl[pl.ds(i, ROWS, stride=16), :] = high
                 kl[pl.ds(i + 4, ROWS, stride=16), :] = high
                 kl[pl.ds(i + 8, ROWS, stride=16), :] = low
                 kl[pl.ds(i + 12, ROWS, stride=16), :] = jnp.zeros_like(low)
+
+        for part in range(2):
+            kq2[:, pl.ds(part * DK, DK)] = kq3[part]
 
     def prepare_gates():
         shape = (ROWS, DV)
@@ -245,6 +253,15 @@
                 gate = g32[:, t, pl.ds(h * DV, DV)]
                 gs[h, t] = gain[...] * gate / (1.0 + jnp.exp(-gate))
 
+    def columns(b, cr):
+        return pl.ds(pl.multiple_of((2 * b + cr) * 128, 128), 128)
+
+    def weights_over():
+        return tc(wout, wgot, wsem.at[0], wsem.at[1], partner)
+
+    def hidden_over(h):
+        return tc(hout.at[h], hgot.at[h], s1.at[h], r1.at[h], partner)
+
     def forward(zp):
         rc(blk(xm, zp, 0), blk(xm, zp, 0), fsp.at[zp], xrp.at[zp, 0], xp, z).wait_recv()
         f_plus(zp).start()
@@ -323,6 +340,19 @@
 
         lax.fori_loop(rank_at(4 * s), rank_at(4 * s + 4), onward, 0)
 
+        @pl.when(s == 3)
+        def _():
+            for b in range(8):
+                wout[b] = weight[:, columns(b, 1 - core)].astype(F32)
+                wall[b, pl.ds(0, HEADS * DV)] = weight[:, columns(b, core)]
+            weights_over().start()
+
+        @pl.when(s == 6)
+        def _():
+            weights_over().wait()
+            for b in range(8):
+                wall[b, pl.ds(HEADS * DV, HEADS * DV)] = wgot[b].astype(BF16)
+
         @pl.when(s == 1)
         def _():
             prepare_keys()
@@ -352,16 +382,16 @@
 
     def recall(r, carry):
         high, low = split(state_of(r))
+        halves = jnp.concatenate([high.astype(BF16), low.astype(BF16)], axis=1)
         both = kq2[pl.ds(pl.multiple_of(r * 16, 16), 16), :].astype(BF16)
-        a = lax.dot_general(both, high.astype(BF16), contract, preferred_element_type=F32)
-        b = lax.dot_general(both, low.astype(BF16), contract, preferred_element_type=F32)
-        total = a[0:8] + a[8:16] + b[0:8]
+        a = lax.dot_general(both, halves, contract, preferred_element_type=F32)
+        total = a[0:8] + a[8:16]
         at = pl.ds(pl.multiple_of(r * 8, 8), 8)
         gk[0, at, :] = total[:, 0:DV]
         gk[1, at, :] = total[:, DV:]
         return carry
 
-    lax.fori_loop(0, ROWS, recall, 0, unroll=8)
+    lax.fori_loop(0, ROWS, recall, 0, unroll=16)
 
     def run_steps(h, carry):
         lanes = pl.ds(pl.multiple_of(h * DV, DV), DV)
@@ -376,7 +406,11 @@
             for s in range(t + 1):
                 out = out + cd[h, PAIRS.index((s, t))] * u[s]
             scale = lax.rsqrt(jnp.mean(out * out, axis=1, keepdims=True) + 1e-6)
-            hid[pl.ds(t * ROWS, ROWS), lanes] = (out * scale * gs[h, t]).astype(BF16)
+            some = pl.ds(t * ROWS, ROWS)
+            hidden = (out * scale * gs[h, t]).astype(BF16)
+            hid[some, lanes] = hidden
+            hout[h, some] = hidden.astype(F32)
+        hidden_over(h).start()
         for s in range(STEPS):
             high, low = split(ce[h, s] * u[s])
             wl[h, pl.ds(s, ROWS, stride=16), :] = high
@@ -387,10 +421,6 @@
 
     lax.fori_loop(0, HEADS, run_steps, 0)
 
-    def cross(side, c, yy):
-        at = (side, c, yy)
-        return tc(part.at[at], got1.at[at], s1.at[at], r1.at[at], partner)
-
     def along_y(side, c, hop):
         at = (side, c, hop - 1)
         return tc(
@@ -401,53 +431,24 @@
     def along_z(c):
         return tc(acc.at[c], got3.at[c], s3.at[c], r3.at[c], far)
 
+    for h in range(HEADS):
+        hidden_over(h).wait_recv()
+        hid[:, pl.ds((HEADS + h) * DV, DV)] = hgot[h].astype(BF16)
+
     def product(n, carry):
         side = n // 4
-        yy = (y + 1 + n) % 4
+        hop = (n + 2) % 4
+        yy = (y + hop) % 4
         zz = (zh + 1 + side) % 2
-        at = pl.multiple_of((yy * 2 + zz) * 256, 256)
-        both = jnp.dot(hid[...], weight[:, pl.ds(at, 256)], preferred_element_type=F32)
-        theirs = jnp.where(core == 0, both[:, 128:], both[:, :128])
-        ours = jnp.where(core == 0, both[:, :128], both[:, 128:])
+        term = jnp.dot(hid[...], wall[yy * 2 + zz], preferred_element_type=F32)
         for c in range(CHUNKS):
-            part[side, c, yy] = theirs[c * CROWS : (c + 1) * CROWS]
-            mine[side, c, yy] = ours[c * CROWS : (c + 1) * CROWS]
-            cross(side, c, yy).start()
-        return carry
-
-    lax.fori_loop(0, 8, product, 0)
-
-    def merge(n, carry):
-        side = n // (4 * CHUNKS)
-        c = (n // 4) % CHUNKS
-        hop = (n + 1) % 4
-        yy = (y + hop) % 4
-        cross(side, c, yy).wait_recv()
-        mine[side, c, yy] = mine[side, c, yy] + got1[side, c, yy]
-
-        @pl.when(hop > 0)
-        def _():
-            along_y(side, c, hop).start()
-
-        return carry
-
-    lax.fori_loop(0, 8 * CHUNKS, merge, 0)
-
-    def summed(side, c):
-        for hop in (1, 2, 3):
-            along_y(side, c, hop).wait_recv()
-        return mine[side, c, y] + got2[side, c, 0] + got2[side, c, 1] + got2[side, c, 2]
-
-    @pl.when(zh == 0)
-    def _():
-        pl.semaphore_wait(far_in, 1)
-
-    def send_z(c, carry):
-        acc[c] = summed(0, c)
-        along_z(c).start()
-        return carry
-
-    lax.fori_loop(0, CHUNKS, send_z, 0)
+            mine[side, c, yy] = term[c * CROWS : (c + 1) * CROWS]
+
+            @pl.when(hop > 0)
+            def _():
+                along_y(side, c, hop).start()
+
+        return carry
 
     def finish(r, carry):
         state = state_of(r)
@@ -464,7 +465,28 @@
             ).astype(BF16)
         return carry
 
-    lax.fori_loop(0, ROWS, finish, 0)
+    lax.fori_loop(0, 4, product, 0)
+    early = jnp.where(z < 4, 12, 12)
+    lax.fori_loop(0, early, finish, 0)
+
+    def summed(side, c):
+        for hop in (1, 2, 3):
+            along_y(side, c, hop).wait_recv()
+        return mine[side, c, y] + got2[side, c, 0] + got2[side, c, 1] + got2[side, c, 2]
+
+    @pl.when(zh == 0)
+    def _():
+        pl.semaphore_wait(far_in, 1)
+
+    def send_z(c, carry):
+        acc[c] = summed(0, c)
+        along_z(c).start()
+        return carry
+
+    lax.fori_loop(0, CHUNKS, send_z, 0)
+
+    lax.fori_loop(4, 8, product, 0)
+    lax.fori_loop(early, ROWS, finish, 0)
 
     t_plus(tail(x)).wait_send()
     t_minus(tail(x)).wait_send()
@@ -499,13 +521,13 @@
     lax.fori_loop(0, NZ, sent, 0)
 
     def left(n, carry):
-        for yy in range(4):
-            cross(n // CHUNKS, n % CHUNKS, yy).wait_send()
         for hop in (1, 2, 3):
             along_y(n // CHUNKS, n % CHUNKS, hop).wait_send()
         return carry
 
     lax.fori_loop(0, 2 * CHUNKS, left, 0)
+    for h in range(HEADS):
+        hidden_over(h).wait_send()
 
     def keep(c, carry):
         near[c] = summed(1, c)
@@ -590,7 +612,8 @@
             pltpu.VMEM((ROWS, STEPS, HEADS * DV), F32),
             pltpu.VMEM((STEPS * 2 * HEADS, 128), F32),
             pltpu.VMEM((2 * STEPS, ROWS, DK), F32),
-            pltpu.VMEM((ROWS * 16, DK), F32),
+            pltpu.VMEM((ROWS * 16, 2 * DK), F32),
+            pltpu.VMEM((2, ROWS * 16, DK), F32),
             pltpu.VMEM((ROWS * 16, DK), F32),
             pltpu.VMEM((HEADS, STEPS, ROWS, DV), F32),
             pltpu.VMEM((HEADS, STEPS, ROWS, DV), F32),
@@ -600,9 +623,12 @@
             pltpu.VMEM((HEADS, STEPS, ROWS, DV), F32),
             pltpu.VMEM((HEADS, ROWS * 8, DV), F32),
             pltpu.VMEM((HEADS, ROWS * 16, DV), F32),
-            pltpu.VMEM((ROWS * STEPS, HEADS * DV), BF16),
-            pltpu.VMEM((2, CHUNKS, 4, CROWS, 128), F32),
-            pltpu.VMEM((2, CHUNKS, 4, CROWS, 128), F32),
+            pltpu.VMEM((ROWS * STEPS, 2 * HEADS * DV), BF16),
+            pltpu.VMEM((8, HEADS * DV, 128), F32),
+            pltpu.VMEM((8, HEADS * DV, 128), F32),
+            pltpu.VMEM((8, 2 * HEADS * DV, 128), BF16),
+            pltpu.VMEM((HEADS, ROWS * STEPS, DV), F32),
+            pltpu.VMEM((HEADS, ROWS * STEPS, DV), F32),
             pltpu.VMEM((2, CHUNKS, 4, CROWS, 128), F32),
             pltpu.VMEM((2, CHUNKS, 3, CROWS, 128), F32),
             pltpu.VMEM((CHUNKS, CROWS, 128), F32),
@@ -612,7 +638,7 @@
         ]
         + [dma((NZ, 2)) for _ in range(8)]
         + [dma((NZ,)), dma((NZ,)), dma((4,)), dma((4,)), dma((NZ,)), dma((NZ,)), dma((NZ,))]
-        + [dma((2, CHUNKS, 4)), dma((2, CHUNKS, 4)), dma((2, CHUNKS, 3)), dma((2, CHUNKS, 3))]
+        + [dma((2,)), dma((HEADS,)), dma((HEADS,)), dma((2, CHUNKS, 3)), dma((2, CHUNKS, 3))]
         + [dma((CHUNKS,)), dma((CHUNKS,)), dma, dma((10,)), pltpu.SemaphoreType.REGULAR],
         compiler_params=pltpu.CompilerParams(
             collective_id=0, has_side_effects=True, vmem_limit_bytes=32 * 2**20

time: 95.6 us -> 95.4 us (level)
  no operation moved by 1% of the time
where the time goes in v4:
time: 95.4 us; the launch traced here: 93.9 us
  Pallas kernels  93.3 us (98%)
    pallas_call x1, Pallas kernels, body(): pl.pallas_call(kernel, out_shape=(pltpu.VMEM((ROWS, STEPS, 128), BF16), p...  91.9 us

profile of v4, /device:TPU:6, one launch (start us, length us, event | category | flops | bytes accessed | tf_op | source)
XLA Modules:
  0.0 93.9 jit_solution(17128394746961950604)
XLA Ops:
  0.6 91.9 %shard_map.122 = (bf16[32,4,128]{2,1,0:T(4,128)(2,1)S(1)}, bf16[32,256,128]{2,1,0:T(8,128)(2,1)S(1)}) custom-call(f32[2,256,128]{2,1,0:T(8,128)} %bitcast.4, s32[32]{0:T(128)} %slot_in.1, bf16[32,4,128]{2,1,0:T(4,128)(2,1)} %q_in.1, bf16[32,4,128]{2,1,0:T(4,128)(2,1)} %k_in.1, bf16[32,4,256]{2,1,0:T(4,128)(2,1)} %v_in.1, bf16[32,4,256]{2,1,0:T(4,128)(2,1)} %gate_in.1, ...), custom_call_target="tpu_custom_call" | custom-call | tf_op jit(solution)/shard_map/pallas_call | solution.py:589
  92.6 1.4 %shard_map.123 = (bf16[32,4,128]{2,1,0:T(4,128)(2,1)}, bf16[32,256,128]{2,1,0:T(8,128)(2,1)}) custom-call(bf16[32,4,128]{2,1,0:T(4,128)(2,1)S(1)} %get-tuple-element.6.mixed_in, bf16[32,256,128]{2,1,0:T(8,128)(2,1)S(1)} %get-tuple-element.7.final_in), custom_call_target="tpu_custom_call" | custom-call | tf_op jit(solution)/shard_map/pallas_call | solution.py:647
